TPU v7x, 32 devices: a whole 2x2x4 slice. The times are simulated.
32 devices in a mesh: grp: 2 (over x), feat: 4 (over y, core), hid: 4 (over z).
Axes of the slice: x: 2, y: 2, z: 4, core: 2. Of those that a mesh axis runs over, the one named last changes fastest.
Arguments:
- decoder: bfloat16 [32768, 4096], P(('grp', 'feat'), 'hid'), parts along dimension 0, may hold values from -6 to 6
- encoder: bfloat16 [4096, 32768], P('hid', ('grp', 'feat')), parts along dimension 1, may hold values from -0.09375 to 0.09375
- panel_rows: int32 [8, 4, 4], P(('grp', 'feat')), parts along dimension 0, may hold values from 0 to 31, as said below
- pair_panel: int32 [8, 4, 10], P(('grp', 'feat')), parts along dimension 0, may hold values from 0 to 3
- pair_cols: int32 [8, 4, 10], P(('grp', 'feat')), parts along dimension 0, may hold values from 0 to 31, as said below
- pair_counts: int32 [8, 4], P(('grp', 'feat')), parts along dimension 0, may hold values from 3 to 10, as said below
Outputs:
- virtual_blocks: float32 [320, 128, 128], P(('grp', 'feat', 'hid')), parts along dimension 0
There are 2 independent parts, one for each index of `grp`. A program takes and returns all parts, laid end to end along the dimension named above; each array names one. Nothing has to cross between parts.
Inputs may be any that keep to these rules, and one draw needn't show every extreme that they name: `panel_rows`: within one group (d, s) the 4 entries are different. `pair_cols`: within one group (d, s) the 10 entries are different. `pair_counts`: every column shard d has some group with all 10 slots live.
All inputs are finite; a program needn't handle non-finite values.
Results may differ from a plain program's by a relative error of at most 0.0003.
Values may be sent and summed in bfloat16 or wider, within the bound.
A program may use at most 192 MiB of HBM per device.

v0:
```python
import functools

import jax
import jax.numpy as jnp
from jax import lax
from jax.experimental import pallas as pl
from jax.experimental.pallas import tpu as pltpu
from jax.sharding import PartitionSpec as P

BLK = 128
MESH = pl.DeviceIdType.MESH


def kernel(feats, hids, dec_hbm, enc_hbm, panel_v, panel_s, pick_s, cols_s, count_s, out_ref,
           dec, enc, stocks, outgoing, asked_v, asked_s, part, relay, extra,
           local_sem, strip_sem, ask_send, ask_recv, row_send, row_recv, z_send, z_recv, x_recv):
    pair = 2 if feats % 2 == 0 else 1
    tall = feats // pair
    groups = feats // hids
    cap = panel_s.shape[2]
    slots = pick_s.shape[2]
    step = part.shape[2]
    pieces = slots // step
    me, hid = lax.axis_index("feat"), lax.axis_index("hid")
    chip, core = me // pair, me % pair

    def target(k):
        return ((chip + k // pair) % tall) * pair + (core + k % pair) % pair

    def source(k):
        return ((chip + tall - k // pair) % tall) * pair + (core + pair - k % pair) % pair

    def back(k):
        return ((tall - k // pair) % tall) * pair + (pair - k % pair) % pair

    dec_copy = pltpu.make_async_copy(dec_hbm, dec, local_sem.at[0])
    dec_copy.start()

    def strip(c):
        col = pl.multiple_of(c * BLK, BLK)
        return pltpu.make_async_copy(enc_hbm.at[:, pl.ds(col, BLK)], enc.at[c], strip_sem.at[c])

    @pl.loop(0, enc.shape[0])
    def _(c):
        strip(c).start()

    barrier = pltpu.get_barrier_semaphore()

    @pl.loop(1, feats)
    def _(k):
        pl.semaphore_signal(barrier, inc=1, device_id={"feat": target(k)}, device_id_type=MESH)

    @pl.when(hid > 0)
    def _():
        pl.semaphore_signal(barrier, inc=1, device_id={"hid": hid - 1}, device_id_type=MESH)

    @pl.when(hid < hids - 1)
    def _():
        pl.semaphore_signal(barrier, inc=1, device_id={"hid": hid + 1}, device_id_type=MESH)

    lower = jnp.where(hid > 0, 1, 0)
    upper = jnp.where(hid < hids - 1, 1, 0)
    pl.semaphore_wait(barrier, feats - 1 + lower + upper)

    def ask(k):
        return pltpu.make_async_remote_copy(
            panel_v.at[0], asked_v.at[k], ask_send.at[k], ask_recv.at[k],
            device_id={"feat": target(k)}, device_id_type=MESH)

    def rows(k):
        return pltpu.make_async_remote_copy(
            outgoing.at[k], stocks[k], row_send.at[k], row_recv.at[k],
            device_id={"feat": target(k)}, device_id_type=MESH)

    @pl.loop(1, feats)
    def _(k):
        ask(k).start()

    dec_copy.wait()

    @pl.loop(1, feats)
    def _(k):
        ask(k).wait_recv()

    to_scalar = pltpu.make_async_copy(asked_v, asked_s, local_sem.at[1])
    to_scalar.start()
    to_scalar.wait()

    def ship(k):
        for j in range(cap):
            outgoing[k, j] = dec[asked_s[back(k), me, j]]
        rows(k).start()

    for k in list(range(pair, feats)) + list(range(1, pair)):
        ship(k)
    for j in range(cap):
        stocks[0][j] = dec[panel_s[0, me, j]]

    @pl.loop(0, enc.shape[0])
    def _(c):
        strip(c).wait()

    def pass_on(k, p, landing, sem, neighbour):
        return pltpu.make_async_remote_copy(
            part.at[k, p], landing, z_send.at[k, p], sem,
            device_id={"hid": neighbour}, device_id_type=MESH)

    def take_round(k):
        origin = source(k)
        owner = origin // groups
        mine = origin % groups

        if k > 0:
            rows(k).wait_recv()

        @pl.loop(0, pieces)
        def _(p):
            for i in range(step):
                slot = p * step + i
                live = jnp.minimum(jnp.maximum(count_s[0, origin] - slot, 0), 1)
                part[k, p, i] = live.astype(jnp.float32) * jnp.dot(
                    stocks[k][pick_s[0, origin, slot]], enc[cols_s[0, origin, slot]],
                    preferred_element_type=jnp.float32)

            @pl.when((hid > 0) & (hid <= owner))
            def _():
                pass_on(k, p, relay.at[k, p], z_recv.at[k, p], hid - 1).wait_recv()
                part[k, p] += relay[k, p]

            @pl.when((hid < hids - 1) & (hid > owner))
            def _():
                pass_on(k, p, relay.at[k, p], z_recv.at[k, p], hid + 1).wait_recv()
                part[k, p] += relay[k, p]

            @pl.when((hid < hids - 1) & (hid == owner))
            def _():
                pass_on(k, p, extra.at[mine, p], x_recv.at[mine, p], hid + 1).wait_recv()
                part[k, p] += extra[mine, p]

            @pl.when(hid < owner)
            def _():
                pass_on(k, p, relay.at[k, p], z_recv.at[k, p], hid + 1).start()

            @pl.when(hid > owner + 1)
            def _():
                pass_on(k, p, relay.at[k, p], z_recv.at[k, p], hid - 1).start()

            @pl.when(hid == owner + 1)
            def _():
                pass_on(k, p, extra.at[mine, p], x_recv.at[mine, p], hid - 1).start()

            @pl.when(hid == owner)
            def _():
                out_ref[pl.ds(mine * slots + p * step, step)] = part[k, p]

    for k in range(feats):
        take_round(k)

    for k in range(1, feats):
        ask(k).wait_send()
        rows(k).wait_send()

    @pl.loop(0, feats)
    def _(k):
        owner = source(k) // groups

        @pl.loop(0, pieces)
        def _(p):
            @pl.when(hid < owner)
            def _():
                pass_on(k, p, relay.at[k, p], z_recv.at[k, p], hid + 1).wait_send()

            @pl.when(hid > owner)
            def _():
                pass_on(k, p, relay.at[k, p], z_recv.at[k, p], hid - 1).wait_send()


def on_device(feats, hids, decoder, encoder, panel_rows, pair_panel, pair_cols, pair_counts):
    width = decoder.shape[1]
    blocks, strips = decoder.shape[0] // BLK, encoder.shape[1] // BLK
    cap = panel_rows.shape[2]
    slots = pair_panel.shape[2]
    step = 2 if slots % 2 == 0 else 1
    pieces = slots // step
    groups = feats // hids
    held = pl.BlockSpec(memory_space=pl.ANY)
    vector = pl.BlockSpec(memory_space=pltpu.VMEM)
    scalar = pl.BlockSpec(memory_space=pltpu.SMEM)
    dma = pltpu.SemaphoreType.DMA
    flops = 2 * feats * slots * BLK * BLK * width
    return pl.pallas_call(
        functools.partial(kernel, feats, hids),
        out_shape=jax.ShapeDtypeStruct((groups * slots, BLK, BLK), jnp.float32),
        in_specs=[held, held, vector, scalar, scalar, scalar, scalar],
        out_specs=vector,
        scratch_shapes=[
            pltpu.VMEM((blocks, BLK, width), decoder.dtype),
            pltpu.VMEM((strips, width, BLK), encoder.dtype),
            [pltpu.VMEM((cap, BLK, width), decoder.dtype) for _ in range(feats)],
            pltpu.VMEM((feats, cap, BLK, width), decoder.dtype),
            pltpu.VMEM((feats, feats, cap), jnp.int32),
            pltpu.SMEM((feats, feats, cap), jnp.int32),
            pltpu.VMEM((feats, pieces, step, BLK, BLK), jnp.float32),
            pltpu.VMEM((feats, pieces, step, BLK, BLK), jnp.float32),
            pltpu.VMEM((groups, pieces, step, BLK, BLK), jnp.float32),
            dma((2,)),
            dma((strips,)),
            dma((feats,)),
            dma((feats,)),
            dma((feats,)),
            dma((feats,)),
            dma((feats, pieces)),
            dma((feats, pieces)),
            dma((groups, pieces)),
        ],
        compiler_params=pltpu.CompilerParams(
            collective_id=0, has_side_effects=True, vmem_limit_bytes=60 * 1024 * 1024),
        cost_estimate=pl.CostEstimate(
            flops=flops, bytes_accessed=2 * decoder.size * 2, transcendentals=0),
    )(decoder.reshape(blocks, BLK, width), encoder, panel_rows, panel_rows, pair_panel, pair_cols, pair_counts)


def solution(mesh):
    placed = (
        P(("grp", "feat"), "hid"),
        P("hid", ("grp", "feat")),
        P(("grp", "feat"), None, None),
        P(("grp", "feat"), None, None),
        P(("grp", "feat"), None, None),
        P(("grp", "feat"), None),
    )
    return jax.shard_map(
        functools.partial(on_device, mesh.shape["feat"], mesh.shape["hid"]),
        mesh=mesh,
        in_specs=placed,
        out_specs=P(("grp", "feat", "hid"), None, None),
        check_vma=False,
    )
```

profile of v0, /device:TPU:17, one launch (start us, length us, event | category | flops | bytes accessed | tf_op | source)
XLA Modules:
  0.0 82.5 jit_solution(7115498298653089541)
XLA Ops:
  0.0 80.5 %shard_map.64 = f32[10,128,128]{2,1,0:T(8,128)} custom-call(bf16[32,128,1024]{2,1,0:T(8,128)(2,1)} %bitcast.1, bf16[1024,4096]{1,0:T(8,128)(2,1)} %enc_hbm.1, s32[1,4,4]{2,1,0:T(4,128)} %panel_s.1, s32[1,4,4]{2,1,0:T(4,128)} %panel_s.1, s32[1,4,10]{2,1,0:T(4,128)} %pick_s.1, s32[1,4,10]{2,1,0:T(4,128)} %cols_s.1, s32[1,4]{1,0:T(1,128)} %count_s.1), custom_call_target="tpu_custom_call" | custom-call | flops 1342177280 | bytes 16777216 | tf_op jit(solution)/shard_map/pallas_call | solution.py:191
  80.5 2.0 %copy.8 = f32[10,128,128]{2,1,0:T(8,128)} copy(f32[10,128,128]{2,1,0:T(8,128)} %shard_map.64) | data formatting | bytes 1310720
where the time goes:
time: 82.7 us; the launch traced here: 82.5 us
  Pallas kernels  80.5 us (97%)
  local copies, waits for them, and re-layouts  1.97 us (2%)
    pallas_call x1, Pallas kernels, on_device(): pl.pallas_call(functools.partial(kernel, feats, hids), out_shape=jax.Shap...  80.5 us
    unnamed x1, local copies, waits for them, and re-layouts  1.97 us

commit v1 on v0

--- a/solution.py
+++ b/solution.py
@@ -8,6 +8,7 @@
 from jax.sharding import PartitionSpec as P
 
 BLK = 128
+CUTS = 2
 MESH = pl.DeviceIdType.MESH
 
 
@@ -20,6 +21,7 @@
     cap = panel_s.shape[2]
     slots = pick_s.shape[2]
     step = part.shape[2]
+    sub = BLK // CUTS
     pieces = slots // step
     me, hid = lax.axis_index("feat"), lax.axis_index("hid")
     chip, core = me // pair, me % pair
@@ -67,9 +69,10 @@
             panel_v.at[0], asked_v.at[k], ask_send.at[k], ask_recv.at[k],
             device_id={"feat": target(k)}, device_id_type=MESH)
 
-    def rows(k):
+    def rows(k, h):
+        q = k * CUTS + h
         return pltpu.make_async_remote_copy(
-            outgoing.at[k], stocks[k], row_send.at[k], row_recv.at[k],
+            outgoing.at[q], stocks[q], row_send.at[q], row_recv.at[q],
             device_id={"feat": target(k)}, device_id_type=MESH)
 
     @pl.loop(1, feats)
@@ -87,14 +90,16 @@
     to_scalar.wait()
 
     def ship(k):
-        for j in range(cap):
-            outgoing[k, j] = dec[asked_s[back(k), me, j]]
-        rows(k).start()
+        for h in range(CUTS):
+            for j in range(cap):
+                outgoing[k * CUTS + h, j] = dec[asked_s[back(k), me, j], h]
+            rows(k, h).start()
 
     for k in list(range(pair, feats)) + list(range(1, pair)):
         ship(k)
     for j in range(cap):
-        stocks[0][j] = dec[panel_s[0, me, j]]
+        for h in range(CUTS):
+            stocks[h][j] = dec[panel_s[0, me, j], h]
 
     @pl.loop(0, enc.shape[0])
     def _(c):
@@ -105,64 +110,68 @@
             part.at[k, p], landing, z_send.at[k, p], sem,
             device_id={"hid": neighbour}, device_id_type=MESH)
 
-    def take_round(k):
+    def take_round(k, h):
+        q = k * CUTS + h
         origin = source(k)
         owner = origin // groups
         mine = origin % groups
+        kept = mine * CUTS + h
 
         if k > 0:
-            rows(k).wait_recv()
+            rows(k, h).wait_recv()
 
         @pl.loop(0, pieces)
         def _(p):
             for i in range(step):
                 slot = p * step + i
                 live = jnp.minimum(jnp.maximum(count_s[0, origin] - slot, 0), 1)
-                part[k, p, i] = live.astype(jnp.float32) * jnp.dot(
-                    stocks[k][pick_s[0, origin, slot]], enc[cols_s[0, origin, slot]],
+                part[q, p, i] = live.astype(jnp.float32) * jnp.dot(
+                    stocks[q][pick_s[0, origin, slot]], enc[cols_s[0, origin, slot]],
                     preferred_element_type=jnp.float32)
 
             @pl.when((hid > 0) & (hid <= owner))
             def _():
-                pass_on(k, p, relay.at[k, p], z_recv.at[k, p], hid - 1).wait_recv()
-                part[k, p] += relay[k, p]
+                pass_on(q, p, relay.at[q, p], z_recv.at[q, p], hid - 1).wait_recv()
+                part[q, p] += relay[q, p]
 
             @pl.when((hid < hids - 1) & (hid > owner))
             def _():
-                pass_on(k, p, relay.at[k, p], z_recv.at[k, p], hid + 1).wait_recv()
-                part[k, p] += relay[k, p]
+                pass_on(q, p, relay.at[q, p], z_recv.at[q, p], hid + 1).wait_recv()
+                part[q, p] += relay[q, p]
 
             @pl.when((hid < hids - 1) & (hid == owner))
             def _():
-                pass_on(k, p, extra.at[mine, p], x_recv.at[mine, p], hid + 1).wait_recv()
-                part[k, p] += extra[mine, p]
+                pass_on(q, p, extra.at[kept, p], x_recv.at[kept, p], hid + 1).wait_recv()
+                part[q, p] += extra[kept, p]
 
             @pl.when(hid < owner)
             def _():
-                pass_on(k, p, relay.at[k, p], z_recv.at[k, p], hid + 1).start()
+                pass_on(q, p, relay.at[q, p], z_recv.at[q, p], hid + 1).start()
 
             @pl.when(hid > owner + 1)
             def _():
-                pass_on(k, p, relay.at[k, p], z_recv.at[k, p], hid - 1).start()
+                pass_on(q, p, relay.at[q, p], z_recv.at[q, p], hid - 1).start()
 
             @pl.when(hid == owner + 1)
             def _():
-                pass_on(k, p, extra.at[mine, p], x_recv.at[mine, p], hid - 1).start()
+                pass_on(q, p, extra.at[kept, p], x_recv.at[kept, p], hid - 1).start()
 
             @pl.when(hid == owner)
             def _():
-                out_ref[pl.ds(mine * slots + p * step, step)] = part[k, p]
+                out_ref[pl.ds(mine * slots + p * step, step), h * sub:(h + 1) * sub] = part[q, p]
 
     for k in range(feats):
-        take_round(k)
+        for h in range(CUTS):
+            take_round(k, h)
 
     for k in range(1, feats):
         ask(k).wait_send()
-        rows(k).wait_send()
-
-    @pl.loop(0, feats)
-    def _(k):
-        owner = source(k) // groups
+        for h in range(CUTS):
+            rows(k, h).wait_send()
+
+    @pl.loop(0, feats * CUTS)
+    def _(k):
+        owner = source(k // CUTS) // groups
 
         @pl.loop(0, pieces)
         def _(p):
@@ -183,6 +192,7 @@
     step = 2 if slots % 2 == 0 else 1
     pieces = slots // step
     groups = feats // hids
+    sub = BLK // CUTS
     held = pl.BlockSpec(memory_space=pl.ANY)
     vector = pl.BlockSpec(memory_space=pltpu.VMEM)
     scalar = pl.BlockSpec(memory_space=pltpu.SMEM)
@@ -194,30 +204,30 @@
         in_specs=[held, held, vector, scalar, scalar, scalar, scalar],
         out_specs=vector,
         scratch_shapes=[
-            pltpu.VMEM((blocks, BLK, width), decoder.dtype),
+            pltpu.VMEM((blocks, CUTS, sub, width), decoder.dtype),
             pltpu.VMEM((strips, width, BLK), encoder.dtype),
-            [pltpu.VMEM((cap, BLK, width), decoder.dtype) for _ in range(feats)],
-            pltpu.VMEM((feats, cap, BLK, width), decoder.dtype),
+            [pltpu.VMEM((cap, sub, width), decoder.dtype) for _ in range(feats * CUTS)],
+            pltpu.VMEM((feats * CUTS, cap, sub, width), decoder.dtype),
             pltpu.VMEM((feats, feats, cap), jnp.int32),
             pltpu.SMEM((feats, feats, cap), jnp.int32),
-            pltpu.VMEM((feats, pieces, step, BLK, BLK), jnp.float32),
-            pltpu.VMEM((feats, pieces, step, BLK, BLK), jnp.float32),
-            pltpu.VMEM((groups, pieces, step, BLK, BLK), jnp.float32),
+            pltpu.VMEM((feats * CUTS, pieces, step, sub, BLK), jnp.float32),
+            pltpu.VMEM((feats * CUTS, pieces, step, sub, BLK), jnp.float32),
+            pltpu.VMEM((groups * CUTS, pieces, step, sub, BLK), jnp.float32),
             dma((2,)),
             dma((strips,)),
             dma((feats,)),
             dma((feats,)),
-            dma((feats,)),
-            dma((feats,)),
-            dma((feats, pieces)),
-            dma((feats, pieces)),
-            dma((groups, pieces)),
+            dma((feats * CUTS,)),
+            dma((feats * CUTS,)),
+            dma((feats * CUTS, pieces)),
+            dma((feats * CUTS, pieces)),
+            dma((groups * CUTS, pieces)),
         ],
         compiler_params=pltpu.CompilerParams(
             collective_id=0, has_side_effects=True, vmem_limit_bytes=60 * 1024 * 1024),
         cost_estimate=pl.CostEstimate(
             flops=flops, bytes_accessed=2 * decoder.size * 2, transcendentals=0),
-    )(decoder.reshape(blocks, BLK, width), encoder, panel_rows, panel_rows, pair_panel, pair_cols, pair_counts)
+    )(decoder.reshape(blocks, CUTS, sub, width), encoder, panel_rows, panel_rows, pair_panel, pair_cols, pair_counts)
 
 
 def solution(mesh):

time: 82.7 us -> 78.7 us (0.952)
  Pallas kernels: 80.5 us -> 76.5 us
    pallas_call x1, Pallas kernels: 80.5 us -> 76.5 us  [on_device(): pl.pallas_call(functools.partial(kernel, feats, hids), out_shape=jax.Shap...]
where the time goes in v1:
time: 78.7 us; the launch traced here: 78.5 us
  Pallas kernels  76.5 us (97%)
  local copies, waits for them, and re-layouts  1.97 us (3%)
    pallas_call x1, Pallas kernels, on_device(): pl.pallas_call(functools.partial(kernel, feats, hids), out_shape=jax.Shap...  76.5 us
    unnamed x1, local copies, waits for them, and re-layouts  1.97 us

profile of v1, /device:TPU:17, one launch (start us, length us, event | category | flops | bytes accessed | tf_op | source)
XLA Modules:
  0.0 78.5 jit_solution(3484057777478175376)
XLA Ops:
  0.0 76.5 %shard_map.64 = f32[10,128,128]{2,1,0:T(8,128)} custom-call(bf16[32,2,64,1024]{3,2,1,0:T(8,128)(2,1)} %bitcast.1, bf16[1024,4096]{1,0:T(8,128)(2,1)} %enc_hbm.1, s32[1,4,4]{2,1,0:T(4,128)} %panel_s.1, s32[1,4,4]{2,1,0:T(4,128)} %panel_s.1, s32[1,4,10]{2,1,0:T(4,128)} %pick_s.1, s32[1,4,10]{2,1,0:T(4,128)} %cols_s.1, s32[1,4]{1,0:T(1,128)} %count_s.1), custom_call_target="tpu_custom_call" | custom-call | flops 1342177280 | bytes 16777216 | tf_op jit(solution)/shard_map/pallas_call | solution.py:201
  76.5 2.0 %copy.8 = f32[10,128,128]{2,1,0:T(8,128)} copy(f32[10,128,128]{2,1,0:T(8,128)} %shard_map.64) | data formatting | bytes 1310720

commit v2 on v1

--- a/solution.py
+++ b/solution.py
@@ -117,11 +117,15 @@
         mine = origin % groups
         kept = mine * CUTS + h
 
-        if k > 0:
-            rows(k, h).wait_recv()
-
-        @pl.loop(0, pieces)
-        def _(p):
+        inward = jnp.where(hid > owner, hids - 1 - hid, hid)
+        lag = jnp.where(hid == owner, jnp.maximum(hid, hids - 1 - hid), inward)
+
+        def take_piece(p):
+            if k > 0:
+                @pl.when(p == 0)
+                def _():
+                    rows(k, h).wait_recv()
+
             for i in range(step):
                 slot = p * step + i
                 live = jnp.minimum(jnp.maximum(count_s[0, origin] - slot, 0), 1)
@@ -160,9 +164,20 @@
             def _():
                 out_ref[pl.ds(mine * slots + p * step, step), h * sub:(h + 1) * sub] = part[q, p]
 
-    for k in range(feats):
-        for h in range(CUTS):
-            take_round(k, h)
+        return lag, take_piece
+
+    turns = [take_round(k, h) for k in range(feats) for h in range(CUTS)]
+    starts = [q * pieces for q in range(feats * CUTS)]
+
+    @pl.loop(0, starts[-1] + pieces + hids - 1)
+    def _(t):
+        for q in range(feats * CUTS):
+            lag, take_piece = turns[q]
+            p = t - starts[q] - lag
+
+            @pl.when((p >= 0) & (p < pieces))
+            def _():
+                take_piece(p)
 
     for k in range(1, feats):
         ask(k).wait_send()

time: 78.7 us -> 77.9 us (0.990); the launches traced: 78.5 us -> 76.5 us
  Pallas kernels: 76.5 us -> 74.5 us
    pallas_call x1, Pallas kernels: 76.5 us -> 74.5 us  [on_device(): pl.pallas_call(functools.partial(kernel, feats, hids), out_shape=jax.Shap...]
where the time goes in v2:
time: 77.9 us; the launch traced here: 76.5 us
  Pallas kernels  74.5 us (96%)
  local copies, waits for them, and re-layouts  1.97 us (3%)
    pallas_call x1, Pallas kernels, on_device(): pl.pallas_call(functools.partial(kernel, feats, hids), out_shape=jax.Shap...  74.5 us
    unnamed x1, local copies, waits for them, and re-layouts  1.97 us

profile of v2, /device:TPU:17, one launch (start us, length us, event | category | flops | bytes accessed | tf_op | source)
XLA Modules:
  0.0 76.5 jit_solution(4474654913120968080)
XLA Ops:
  0.0 74.5 %shard_map.64 = f32[10,128,128]{2,1,0:T(8,128)} custom-call(bf16[32,2,64,1024]{3,2,1,0:T(8,128)(2,1)} %bitcast.1, bf16[1024,4096]{1,0:T(8,128)(2,1)} %enc_hbm.1, s32[1,4,4]{2,1,0:T(4,128)} %panel_s.1, s32[1,4,4]{2,1,0:T(4,128)} %panel_s.1, s32[1,4,10]{2,1,0:T(4,128)} %pick_s.1, s32[1,4,10]{2,1,0:T(4,128)} %cols_s.1, s32[1,4]{1,0:T(1,128)} %count_s.1), custom_call_target="tpu_custom_call" | custom-call | flops 1342177280 | bytes 16777216 | tf_op jit(solution)/shard_map/pallas_call | solution.py:216
  74.6 2.0 %copy.8 = f32[10,128,128]{2,1,0:T(8,128)} copy(f32[10,128,128]{2,1,0:T(8,128)} %shard_map.64) | data formatting | bytes 1310720
